TPU v7x, 128 devices: a whole 4x4x4 slice. The times are simulated.
128 devices in a mesh: cmp: 4 (over z_lo, core), task: 32 (over x, z_hi, y).
Axes of the slice: x: 4, y: 4, z: 4 (z_hi: 2, z_lo: 2; z = z_hi * 2 + z_lo), core: 2. Of those that a mesh axis runs over, the one named last changes fastest.
Arguments:
- features: bfloat16 [1024, 16384], P('cmp', 'task'), may hold values from 0 to 2
- w_trunk: bfloat16 [16384, 4096], P('task', 'cmp'), may hold values from -0.046875 to 0.046875
- w_head: bfloat16 [4096, 65536], P(None, 'task'), may hold values from -0.09375 to 0.09375
- bias_trunk: float32 [4096], replicated, may hold values from -3 to 3
- bias_head: float32 [65536], P('task'), may hold values from -4 to 4
- targets: bfloat16 [1024, 65536], P('cmp', 'task'), may hold values from 0 to 1
- block_mask: int32 [2, 128], replicated, may hold values from 0 to 1, as said below
Outputs:
- grad_trunk: float32 [16384, 4096], P('task', 'cmp')
- grad_head: bfloat16 [4096, 65536], P('cmp', 'task')
Inputs may be any that keep to these rules, and one draw needn't show every extreme that they name: `block_mask`: each entry is 0 or 1; entry [0, 0] is 1 and the last entry is 0.
All inputs are finite; a program needn't handle non-finite values.
Results may differ from a plain program's by a relative error of at most 0.011.
Values may be sent and summed in bfloat16 or wider, within the bound.
A program may use at most 128 MiB of HBM per device.

v0:
```python
import jax
import jax.numpy as jnp
from jax import lax
from jax.sharding import PartitionSpec as P

BLOCK = 512


def body(features, w_trunk, w_head, bias_trunk, bias_head, targets, block_mask):
    rows = features.shape[0]
    hid_units = w_head.shape[0]
    task_cols = w_head.shape[1]
    per_dev = task_cols // BLOCK
    scale = 1.0 / (rows * lax.axis_size("cmp")) ** 0.5
    cmp_index = lax.axis_index("cmp")
    task_index = lax.axis_index("task")
    share = hid_units // lax.axis_size("task")
    quarter = hid_units // lax.axis_size("cmp")
    pre_part = jnp.dot(
        features,
        lax.all_gather(w_trunk, "cmp", axis=1, tiled=True),
        preferred_element_type=jnp.float32,
    )
    bias_share = lax.dynamic_slice_in_dim(bias_trunk, task_index * share, share, 0)
    pre_share = lax.psum_scatter(pre_part, "task", scatter_dimension=1, tiled=True) + bias_share
    hidden = lax.all_gather(
        jnp.maximum(pre_share, 0.0).astype(jnp.bfloat16), "task", axis=1, tiled=True
    )
    row_ids = cmp_index * rows + jnp.arange(rows)
    blocks_here = lax.dynamic_slice_in_dim(block_mask, task_index * per_dev, per_dev, 1).astype(
        jnp.float32
    )
    onehot = (row_ids[:, None] // BLOCK == jnp.arange(block_mask.shape[0])[None, :]).astype(
        jnp.float32
    )
    mask_rows = jnp.dot(onehot, blocks_here)
    back_dims = (((1,), (1,)), ((), ()))
    logits = jnp.dot(hidden, w_head, preferred_element_type=jnp.float32) + bias_head
    error = (jax.nn.sigmoid(logits) - targets.astype(jnp.float32)).reshape(rows, per_dev, BLOCK)
    grad_logits = (
        (error * mask_rows[:, :, None] * scale).reshape(rows, task_cols).astype(jnp.bfloat16)
    )
    grad_part = lax.dot_general(grad_logits, w_head, back_dims, preferred_element_type=jnp.float32)
    grad_share = lax.psum_scatter(
        grad_part.astype(jnp.bfloat16), "task", scatter_dimension=1, tiled=True
    ).astype(jnp.float32)
    grad_pre = lax.all_gather(
        jnp.where(pre_share > 0, grad_share, 0.0).astype(jnp.bfloat16), "task", axis=1, tiled=True
    )
    row_dims = (((0,), (0,)), ((), ()))
    trunk_term = lax.dot_general(features, grad_pre, row_dims, preferred_element_type=jnp.float32)
    grad_trunk = lax.psum_scatter(
        trunk_term.astype(jnp.bfloat16), "cmp", scatter_dimension=1, tiled=True
    ).astype(jnp.float32)
    mine = lax.dynamic_slice_in_dim(
        lax.all_gather(hidden, "cmp", axis=0, tiled=True), cmp_index * quarter, quarter, 1
    )
    grad_head = lax.dot_general(
        mine,
        lax.all_gather(grad_logits, "cmp", axis=0, tiled=True),
        row_dims,
        preferred_element_type=jnp.float32,
    )
    return (grad_trunk, grad_head.astype(jnp.bfloat16))


def solution(mesh):
    return jax.shard_map(
        body,
        mesh=mesh,
        in_specs=(
            P("cmp", "task"),
            P("task", "cmp"),
            P(None, "task"),
            P(),
            P("task"),
            P("cmp", "task"),
            P(),
        ),
        out_specs=(P("task", "cmp"), P("cmp", "task")),
        check_vma=False,
    )
```

profile of v0, /device:TPU:1, one launch (start us, length us, event | category | flops | bytes accessed | tf_op | source)
XLA Modules:
  0.0 808.5 jit_solution(6390689914261963847)
XLA Ops:
  7.2 0.7 all-gather.6.cloned.1.call-update
  7.9 0.0 reduce-scatter.6.cloned.1.call-start
  8.0 52.0 %all-gather.6.cloned.1.call-done = bf16[512,4096]{1,0:T(8,128)(2,1)} async-done(((bf16[512,1024]{1,0:T(8,128)(2,1)}), bf16[512,4096]{1,0:T(8,128)(2,1)}) %all-gather.6.cloned.1.call-update) | async-done | bytes 4194320 | tf_op jit(solution)/shard_map/all_gather | solution.py:21
  59.9 5.5 fusion.16
  65.4 0.0 all-gather.8.cloned.1.call-start
  65.5 0.8 dynamic_slice.9
  66.3 169.0 %reduce-scatter.6.cloned.1.call-done = f32[256,128]{1,0:T(8,128)} async-done(((f32[256,4096]{1,0:T(8,128)}), f32[256,128]{1,0:T(8,128)}) %reduce-scatter.6.cloned.1.call-update) | async-done | bytes 131088 | tf_op jit(solution)/shard_map/reduce_scatter | solution.py:25
  235.3 1.5 maximum_convert_fusion
  236.9 0.0 reduce-scatter.10.cloned.1.call-start
  236.9 0.2 fusion.10
  237.2 0.3 mul.33
  237.5 0.9 copy.16
  238.4 94.4 %all-gather.8.cloned.1.call-done = bf16[256,4096]{1,0:T(8,128)(2,1)} async-done(((bf16[256,128]{1,0:T(8,128)(2,1)}), bf16[256,4096]{1,0:T(8,128)(2,1)}) %all-gather.8.cloned.1.call-update) | async-done | bytes 2097168 | tf_op jit(solution)/shard_map/all_gather | solution.py:26
  332.8 11.5 %fusion.8 = bf16[256,2048]{1,0:T(8,128)(2,1)S(1)} fusion(f32[256,2048]{1,0:T(8,128)S(1)} %bitcast.17, bf16[256,4096]{1,0:T(8,128)(2,1)} %all-gather.8.cloned.1.call-done, bf16[4096,2048]{1,0:T(8,128)(2,1)} %param.9, bf16[256,2048]{1,0:T(8,128)(2,1)} %param.12, f32[2048]{0:T(1024)S(1)} %copy-done.4), kind=kOutput, calls=%fused_computation.12 | convolution fusion | flops 4299685888 | bytes 23076864 | tf_op jit(solution)/shard_map/dot_general | solution.py:38
  344.4 8.8 %convolution_convert_fusion.1 = bf16[256,4096]{1,0:T(8,128)(2,1)S(1)} fusion(bf16[256,2048]{1,0:T(8,128)(2,1)S(1)} %fusion.8, bf16[4096,2048]{1,0:T(8,128)(2,1)} %param.9), kind=kOutput, calls=%fused_computation.2 | convolution fusion | flops 4296015872 | bytes 19922944 | tf_op jit(solution)/shard_map/dot_general | solution.py:43
  353.2 2.5 copy.14
  355.7 0.0 all-gather.10.cloned.1.call-start
  355.7 162.9 %reduce-scatter.10.cloned.1.call-done = bf16[128,256]{1,0:T(8,128)(2,1)} async-done(((bf16[4096,256]{1,0:T(8,128)(2,1)}), bf16[128,256]{1,0:T(8,128)(2,1)}) %reduce-scatter.10.cloned.1.call-update) | async-done | bytes 65552
  518.6 0.9 copy.15
  519.6 0.7 select_convert_fusion
  520.2 0.0 all-gather.14.cloned.1.call-start
  520.3 0.5 all-gather.14.cloned.1.call-update
  520.8 0.0 all-gather.12.cloned.1.call-start
  520.9 0.7 all-gather.12.cloned.1.call-update
  521.6 0.2 reduce-scatter.8.cloned.1.call-start
  521.8 95.7 %all-gather.10.cloned.1.call-done = bf16[256,4096]{1,0:T(8,128)(2,1)} async-done(((bf16[256,128]{1,0:T(8,128)(2,1)}), bf16[256,4096]{1,0:T(8,128)(2,1)}) %all-gather.10.cloned.1.call-update) | async-done | bytes 2097168 | tf_op jit(solution)/shard_map/all_gather | solution.py:47
  617.5 4.8 fusion
  622.3 43.9 %all-gather.14.cloned.1.call-done = bf16[1024,2048]{1,0:T(8,128)(2,1)} async-done(((bf16[256,2048]{1,0:T(8,128)(2,1)}), bf16[1024,2048]{1,0:T(8,128)(2,1)}) %all-gather.14.cloned.1.call-update) | async-done | bytes 4194320 | tf_op jit(solution)/shard_map/all_gather | solution.py:60
  666.2 84.1 %all-gather.12.cloned.1.call-done = bf16[1024,4096]{1,0:T(8,128)(2,1)} async-done(((bf16[256,4096]{1,0:T(8,128)(2,1)}), bf16[1024,4096]{1,0:T(8,128)(2,1)}) %all-gather.12.cloned.1.call-update) | async-done | bytes 8388624 | tf_op jit(solution)/shard_map/all_gather | solution.py:56
  750.4 9.4 %convolution_convert_fusion.2 = bf16[1024,2048]{1,0:T(8,128)(2,1)} fusion(bf16[1024,2048]{1,0:T(8,128)(2,1)} %all-gather.14.cloned.1.call-done, bf16[1024,4096]{1,0:T(8,128)(2,1)} %all-gather.12.cloned.1.call-done, s32[]{:T(128)S(6)} %select_n.27), kind=kOutput, calls=%fused_computation.3 | convolution fusion | flops 4297064448 | bytes 10485764 | tf_op jit(solution)/shard_map/dot_general | solution.py:58
  759.8 39.3 %reduce-scatter.8.cloned.1.call-done = bf16[512,1024]{0,1:T(8,128)(2,1)} async-done(((bf16[512,4096]{0,1:T(8,128)(2,1)}), bf16[512,1024]{0,1:T(8,128)(2,1)}) %reduce-scatter.8.cloned.1.call-update) | async-done | bytes 1048592 | tf_op jit(solution)/shard_map/reduce_scatter | solution.py:52
  799.1 2.6 copy.12
  (17 shorter events, 0.2 us)
Async XLA Ops:
  7.2 52.8 %copy-start = (bf16[256,512]{1,0:T(8,128)(2,1)S(1)}, bf16[256,512]{1,0:T(8,128)(2,1)}, u32[]{:S(2)}) copy-start(bf16[256,512]{1,0:T(8,128)(2,1)} %param.7) | copy-start | bytes 786436
  7.2 52.8 %all-gather.6.cloned.1.call-start = ((), (), s32[]{:S(2)}) async-start(), calls=%async_computation.3 | async-start | bytes 5242880 | tf_op jit(solution)/shard_map/all_gather | solution.py:21
  7.9 227.4 %reduce-scatter.6.cloned.1.call-start = ((), (), s32[]{:S(2)}) async-start(), calls=%async_computation.4 | async-start | bytes 4325376 | tf_op jit(solution)/shard_map/reduce_scatter | solution.py:25
  65.4 171.5 %copy-start.3 = (s32[2,128]{1,0:T(2,128)S(1)}, s32[2,128]{1,0:T(2,128)}, u32[]{:S(2)}) copy-start(s32[2,128]{1,0:T(2,128)} %param.13) | copy-start | bytes 3076
  65.4 267.4 %all-gather.8.cloned.1.call-start = ((), (), s32[]{:S(2)}) async-start(), calls=%async_computation.5 | async-start | bytes 2162688 | tf_op jit(solution)/shard_map/all_gather | solution.py:26
  236.9 281.7 %reduce-scatter.10.cloned.1.call-start = ((), (), s32[]{:S(2)}) async-start(), calls=%async_computation.10 | async-start | bytes 2162688
  237.5 95.3 %copy-start.4 = (f32[2048]{0:T(1024)S(1)}, f32[2048]{0:T(1024)}, u32[]{:S(2)}) copy-start(f32[2048]{0:T(1024)} %param.11) | copy-start | bytes 24580
  344.4 8.8 %copy-start.1 = (bf16[256,2048]{1,0:T(8,128)(2,1)}, bf16[256,2048]{1,0:T(8,128)(2,1)S(1)}, u32[]{:S(2)}) copy-start(bf16[256,2048]{1,0:T(8,128)(2,1)S(1)} %fusion.8) | copy-start | bytes 3145732
  355.7 163.9 %copy-start.2 = (f32[256,128]{1,0:T(8,128)S(1)}, f32[256,128]{1,0:T(8,128)}, u32[]{:S(2)}) copy-start(f32[256,128]{1,0:T(8,128)} %reduce-scatter.6.cloned.1.call-done) | copy-start | bytes 393220
  355.7 261.8 %all-gather.10.cloned.1.call-start = ((), (), s32[]{:S(2)}) async-start(), calls=%async_computation.6 | async-start | bytes 2162688 | tf_op jit(solution)/shard_map/all_gather | solution.py:47
  520.2 146.0 %all-gather.14.cloned.1.call-start = ((), (), s32[]{:S(2)}) async-start(), calls=%async_computation.9 | async-start | bytes 5242880 | tf_op jit(solution)/shard_map/all_gather | solution.py:60
  520.8 229.6 %all-gather.12.cloned.1.call-start = ((), (), s32[]{:S(2)}) async-start(), calls=%async_computation.8 | async-start | bytes 10485760 | tf_op jit(solution)/shard_map/all_gather | solution.py:56
  521.6 277.5 %reduce-scatter.8.cloned.1.call-start = ((), (), s32[]{:S(2)}) async-start(), calls=%async_computation.7 | async-start | bytes 5242880 | tf_op jit(solution)/shard_map/reduce_scatter | solution.py:52
Sparse Core Ops, SparseCore 0:
  9.7 50.2 all-gather.5
  65.6 169.6 reduce-scatter.5
  238.6 94.1 all-gather.7
  355.8 162.7 reduce-scatter.9
  522.2 95.2 all-gather.9
  619.7 46.5 all-gather.13
  668.0 82.3 all-gather.11
  752.9 46.1 reduce-scatter.7
where the time goes:
time: 809 us; the launch traced here: 808 us
  waiting for transfers between devices  743 us (92%)
  matrix products  40.2 us (5%)
  between operations  14.2 us (2%)
    reduce_scatter x1, waiting for transfers between devices, body(): lax.psum_scatter(pre_part, 'task', scatter_dimension=1, tiled=True)  169 us
    unnamed x9, waiting for transfers between devices  165 us
    all_gather x1, waiting for transfers between devices, body(): lax.all_gather(jnp.where(pre_share > 0, grad_share, 0.0).astype(jnp.bfloa...  95.7 us
    all_gather x1, waiting for transfers between devices, body(): lax.all_gather(jnp.maximum(pre_share, 0.0).astype(jnp.bfloat16), 'task',...  94.4 us
    all_gather x1, waiting for transfers between devices, body(): lax.all_gather(hidden, 'cmp', axis=0, tiled=True)  84.1 us
    all_gather x1, waiting for transfers between devices, body(): lax.all_gather(w_trunk, 'cmp', axis=1, tiled=True)  52 us
    all_gather x1, waiting for transfers between devices, body(): lax.all_gather(grad_logits, 'cmp', axis=0, tiled=True)  43.9 us
    reduce_scatter x1, waiting for transfers between devices, body(): lax.psum_scatter(trunk_term.astype(jnp.bfloat16), 'cmp', scatter_dimensio...  39.3 us
  transfers between devices with their start and end apart: 8, of which 8 were waited for; matrix products, arithmetic and copies ran while one was open for 2% of the time, Pallas kernels for 0%

commit v1 on v0

v1 whole, which is shorter than its diff:
```python
import jax
import jax.numpy as jnp
from jax import lax
from jax.experimental import pallas as pl
from jax.experimental.pallas import tpu as pltpu
from jax.sharding import PartitionSpec as P

BLOCK = 512
MESH = pl.DeviceIdType.MESH
BF16 = jnp.bfloat16
F32 = jnp.float32


def dot(a, b):
    return jnp.dot(a, b, preferred_element_type=F32)


def dot_t(a, b):
    return lax.dot_general(a, b, (((1,), (1,)), ((), ())), preferred_element_type=F32)


def kernel(
    feat_hbm, wt_hbm, wh_hbm, bt_ref, bh_ref, tg_hbm, mask_ref,
    gt_hbm, gh_hbm,
    wh, wt, wtt, feat, featt, tg,
    p, p_in1, p_s1, p_in2, p_s2, p_in3, pre, pieces,
    h1, h1t, h2, gl, glt,
    q, q_in1, q_s1, q_in2, q_s2, q_in3, back, gpt,
    gh, gt, ssem, rsem, lsem,
):
    c = lax.axis_index("cmp")
    t = lax.axis_index("task")
    x, zh, y = t // 8, (t // 4) % 2, t % 4
    zl, core = c // 2, c % 2
    across_z = (c + 2) % 4
    across_core = c + 1 - 2 * core

    def to_x(d):
        return {"task": ((x + d) % 4) * 8 + zh * 4 + y}

    def to_y(d):
        return {"task": x * 8 + zh * 4 + (y + d) % 4}

    def to_z():
        return {"task": x * 8 + (1 - zh) * 4 + y}

    first, second = (x, y), (y, x)
    to_first, to_second = (to_x, to_y), (to_y, to_x)

    sent = []

    def send(src, dst, device):
        i = len(sent)
        copy = pltpu.make_async_remote_copy(
            src_ref=src, dst_ref=dst, send_sem=ssem.at[i], recv_sem=rsem.at[i],
            device_id=device, device_id_type=MESH,
        )
        copy.start()
        sent.append(copy)
        return copy

    local = []

    def fetch(src, dst):
        copy = pltpu.make_async_copy(src, dst, lsem.at[len(local)])
        copy.start()
        local.append(copy)
        return copy

    def wait_recv(copies):
        for copy in copies:
            copy.wait_recv()

    get_feat = fetch(feat_hbm, feat.at[c])
    get_wt = fetch(wt_hbm, wt)
    get_tg = fetch(tg_hbm, tg)
    get_wh = fetch(wh_hbm, wh)

    barrier = pltpu.get_barrier_semaphore()
    peers = [to_x(d) for d in (1, 2, 3)] + [to_y(d) for d in (1, 2, 3)] + [to_z()]
    peers += [{"cmp": (c + d) % 4} for d in (1, 2, 3)]
    for peer in peers:
        pl.semaphore_signal(barrier, inc=1, device_id=peer, device_id_type=MESH)
    pl.semaphore_wait(barrier, len(peers))

    get_feat.wait()
    f_z = send(feat.at[c], feat.at[c], {"cmp": across_z})
    f_core = send(feat.at[c], feat.at[c], {"cmp": across_core})

    def turn_feat(slot):
        featt[slot // 2, :, pl.ds(pl.multiple_of(slot % 2 * 256, 256), 256)] = feat[slot].T

    turn_feat(c)
    get_wt.wait()

    @pl.loop(0, 4)
    def _(i):
        block = wt[:, pl.ds(pl.multiple_of(i * 256, 256), 256)].T
        wtt[i] = block.reshape(2, 4, 32, 512)

    f_core.wait_recv()
    turn_feat(across_core)

    def pre_tile(ch, i):
        if ch == 0:
            rows = wtt[i].reshape(256, 512)
        else:
            rows = wtt[:, :, i].reshape(256, 512)
        half = zl if ch == 0 else 1 - zl
        out = dot(rows, featt[half])
        if ch == 0:
            out = out.reshape(2, 4, 32, 512)
            for j in range(4):
                for z in range(2):
                    p[ch, i, j, z] = out[z, j]
        else:
            out = out.reshape(4, 2, 32, 512)
            for j in range(4):
                for z in range(2):
                    p[ch, i, j, z] = out[j, z]

    def start_reduce(ch, tile, buf, arrive):
        copies = []
        for d in (2, 1, 3, 0):
            i = (first[ch] + d) % 4
            tile(ch, i)
            if d:
                copies.append(send(buf.at[ch, i], arrive.at[ch, d - 1], to_first[ch](d)))
        return copies

    def add_first(ch, buf, arrive, total):
        @pl.loop(0, 8)
        def _(k):
            j, z = k // 2, k % 2
            value = buf[ch, first[ch], j, z].astype(F32)
            for d in range(3):
                value = value + arrive[ch, d, j, z].astype(F32)
            total[ch, j, z] = value.astype(total.dtype)

    def send_second(ch, total, arrive):
        copies = []
        for d in (2, 1, 3):
            j = (second[ch] + d) % 4
            copies.append(send(total.at[ch, j], arrive.at[ch, d - 1], to_second[ch](d)))
        return copies

    def add_second(ch, total, arrive, out):
        for z in range(2):
            value = total[ch, second[ch], z].astype(F32)
            for d in range(3):
                value = value + arrive[ch, d, z].astype(F32)
            out[ch, z] = value.astype(out.dtype)

    def finish_reduce(copies, buf, in1, s1, in2, s2, in3):
        moves = []
        for ch in range(2):
            wait_recv(copies[ch])
            add_first(ch, buf, in1, s1)
            moves.append(send_second(ch, s1, in2))
        last = []
        for ch in range(2):
            wait_recv(moves[ch])
            add_second(ch, s1, in2, s2)
            last.append(send(s2.at[ch, 1 - zh], in3.at[ch], to_z()))
        out = []
        for ch in range(2):
            last[ch].wait_recv()
            out.append(s2[ch, zh].astype(F32) + in3[ch].astype(F32))
        return out

    def gather_z(ch, buf):
        part = buf.at[ch, first[ch], second[ch], zh]
        return send(part, part, to_z())

    def gather_second(ch, buf):
        part = buf.at[ch, first[ch], second[ch]]
        return [send(part, part, to_second[ch](d)) for d in (2, 1, 3)]

    def gather_first(ch, buf):
        part = buf.at[ch, first[ch]]
        return [send(part, part, to_first[ch](d)) for d in (2, 1, 3)]

    moving0 = start_reduce(0, pre_tile, p, p_in1)
    f_z.wait_recv()
    f_far = send(feat.at[across_z], feat.at[across_z], {"cmp": across_core})
    turn_feat(across_z)
    f_far.wait_recv()
    turn_feat((across_core + 2) % 4)
    moving1 = start_reduce(1, pre_tile, p, p_in1)
    sums = finish_reduce([moving0, moving1], p, p_in1, p_s1, p_in2, p_s2, p_in3)

    row = bt_ref[pl.ds(c * 8 + t // 4, 1), :]
    lane = lax.broadcasted_iota(jnp.int32, (32, 128), 1)
    unit = lax.broadcasted_iota(jnp.int32, (32, 128), 0)
    bias = jnp.sum(
        jnp.where(lane == unit + (t % 4) * 32, jnp.broadcast_to(row, (32, 128)), 0.0),
        axis=1, keepdims=True,
    )
    for ch in range(2):
        half = zl if ch == 0 else 1 - zl
        value = sums[ch] + bias
        pre[half] = value
        value = jnp.maximum(value, 0.0).astype(BF16)
        h2[half, first_of(half, x, y), second_of(half, x, y), zh] = value
        pieces[2 * half] = value[:, :256]
        pieces[2 * half + 1] = value[:, 256:]
    own = c // 2
    slot = h1.at[own, first_of(own, x, y), second_of(own, x, y), zh, core]
    swap = []
    for d in (2, 1, 3):
        swap.append(send(pieces.at[(c + d) % 4], slot, {"cmp": (c + d) % 4}))
    h1[own, first_of(own, x, y), second_of(own, x, y), zh, core] = pieces[c]
    g2z = [gather_z(ch, h2) for ch in range(2)]
    wait_recv(swap)

    g1z = [gather_z(ch, h1) for ch in range(2)]
    g1s = []
    for ch in range(2):
        g1z[ch].wait_recv()
        g1s.append(gather_second(ch, h1))
    g1f = []
    for ch in range(2):
        wait_recv(g1s[ch])
        g1f.append(gather_first(ch, h1))
    g2s = []
    for ch in range(2):
        g2z[ch].wait_recv()
        g2s.append(gather_second(ch, h2))
    for ch in range(2):
        wait_recv(g1f[ch])
    g2f = []
    for ch in range(2):
        wait_recv(g2s[ch])
        g2f.append(gather_first(ch, h2))

    for ch in range(2):
        @pl.loop(0, 8)
        def _(k):
            quarter, i = k // 4, k % 4
            if ch == 0:
                parts = [h1[ch, i, j, z, quarter] for z in range(2) for j in range(4)]
            else:
                parts = [h1[ch, j, i, z, quarter] for z in range(2) for j in range(4)]
            block = jnp.concatenate(parts, axis=0)
            column = pl.multiple_of(ch * 2048 + quarter * 1024 + i * 256, 256)
            h1t[:, pl.ds(column, 256)] = block.T

    get_wh.wait()
    get_tg.wait()

    @pl.loop(0, 4)
    def _(k):
        cols = pl.ds(pl.multiple_of(k * BLOCK, BLOCK), BLOCK)
        logits = dot(h1t[...], wh[:, :, :, :, :, cols].reshape(4096, BLOCK)) + bh_ref[:, cols]
        seen = mask_ref[zl, t * 4 + k].astype(F32)
        error = seen * (jax.nn.sigmoid(logits) - tg[:, cols].astype(F32)) * (1.0 / 32.0)
        error = error.astype(BF16)
        gl[c, :, cols] = error
        glt[cols, :] = error.T

    g_z = send(gl.at[c], gl.at[c], {"cmp": across_z})
    g_core = send(gl.at[c], gl.at[c], {"cmp": across_core})

    def back_tile(ch, i):
        @pl.loop(0, 2)
        def _(quarter):
            if ch == 0:
                rows = wh[ch * 2 + quarter, i].reshape(256, 2048)
            else:
                rows = wh[ch * 2 + quarter, :, :, i].reshape(256, 2048)
            out = dot(rows, glt[...]).astype(BF16)
            if ch == 0:
                out = out.reshape(2, 4, 32, 256)
                for j in range(4):
                    for z in range(2):
                        q[ch, i, j, z, quarter] = out[z, j]
            else:
                out = out.reshape(4, 2, 32, 256)
                for j in range(4):
                    for z in range(2):
                        q[ch, i, j, z, quarter] = out[j, z]

    moving = [start_reduce(ch, back_tile, q, q_in1) for ch in range(2)]
    sums = finish_reduce(moving, q, q_in1, q_s1, q_in2, q_s2, q_in3)

    for ch in range(2):
        for quarter in range(2):
            pieces2 = sums[ch][quarter].astype(BF16)
            back[0, ch * 2 + quarter] = pieces2
    swap = []
    for d in (2, 1, 3):
        swap.append(send(back.at[0, (c + d) % 4], back.at[1, c], {"cmp": (c + d) % 4}))
    back[1, c] = back[0, c]
    wait_recv(swap)
    for half in range(2):
        value = jnp.concatenate([back[1, 2 * half], back[1, 2 * half + 1]], axis=1)
        value = jnp.where(pre[half] > 0.0, value.astype(F32), 0.0).astype(BF16)
        gpt[half, first[half], second[half], zh] = value

    g3z = [gather_z(ch, gpt) for ch in range(2)]
    g3s = []
    for ch in range(2):
        g3z[ch].wait_recv()
        g3s.append(gather_second(ch, gpt))
    g3f = []
    for ch in range(2):
        wait_recv(g3s[ch])
        g3f.append(gather_first(ch, gpt))

    g_z.wait_recv()
    g_far = send(gl.at[across_z], gl.at[across_z], {"cmp": across_core})
    for ch in range(2):
        wait_recv(g2f[ch])
    g_core.wait_recv()
    g_far.wait_recv()

    def unit_tile(buf, ch, i):
        if ch == 0:
            parts = [buf[ch, i, j, z] for z in range(2) for j in range(4)]
        else:
            parts = [buf[ch, j, i, z] for z in range(2) for j in range(4)]
        return jnp.concatenate(parts, axis=0)

    for i in range(4):
        tile = jnp.concatenate([unit_tile(h2, 0, i), unit_tile(h2, 1, i)], axis=1)

        @pl.loop(0, 4)
        def _(k):
            cols = pl.ds(pl.multiple_of(k * 512, 512), 512)
            gh[pl.ds(i * 256, 256), cols] = dot(tile, gl[:, :, cols].reshape(1024, 512)).astype(BF16)

        fetch(gh.at[pl.ds(i * 256, 256)], gh_hbm.at[pl.ds(i * 256, 256)])

    for ch in range(2):
        wait_recv(g3f[ch])
    for i in range(4):
        out = dot_t(featt[0], unit_tile(gpt, 0, i)) + dot_t(featt[1], unit_tile(gpt, 1, i))
        gt[:, i * 256 : (i + 1) * 256] = out
    fetch(gt, gt_hbm)
    for copy in local[4:]:
        copy.wait()
    for copy in sent:
        copy.wait_send()


def first_of(ch, x, y):
    return x * (1 - ch) + y * ch


def second_of(ch, x, y):
    return y * (1 - ch) + x * ch


def body(features, w_trunk, w_head, bias_trunk, bias_head, targets, block_mask):
    hbm = pl.BlockSpec(memory_space=pl.ANY)
    vmem = pl.BlockSpec(memory_space=pltpu.VMEM)
    return pl.pallas_call(
        kernel,
        out_shape=(
            jax.ShapeDtypeStruct((512, 1024), F32),
            jax.ShapeDtypeStruct((1024, 2048), BF16),
        ),
        in_specs=[hbm, hbm, hbm, vmem, vmem, hbm, pl.BlockSpec(memory_space=pltpu.SMEM)],
        out_specs=(hbm, hbm),
        scratch_shapes=[
            pltpu.VMEM((4, 4, 2, 4, 32, 2048), BF16),
            pltpu.VMEM((512, 1024), BF16),
            pltpu.VMEM((4, 2, 4, 32, 512), BF16),
            pltpu.VMEM((4, 256, 512), BF16),
            pltpu.VMEM((2, 512, 512), BF16),
            pltpu.VMEM((256, 2048), BF16),
            pltpu.VMEM((2, 4, 4, 2, 32, 512), F32),
            pltpu.VMEM((2, 3, 4, 2, 32, 512), F32),
            pltpu.VMEM((2, 4, 2, 32, 512), F32),
            pltpu.VMEM((2, 3, 2, 32, 512), F32),
            pltpu.VMEM((2, 2, 32, 512), F32),
            pltpu.VMEM((2, 32, 512), F32),
            pltpu.VMEM((2, 32, 512), F32),
            pltpu.VMEM((4, 32, 256), BF16),
            pltpu.VMEM((2, 4, 4, 2, 2, 32, 256), BF16),
            pltpu.VMEM((256, 4096), BF16),
            pltpu.VMEM((2, 4, 4, 2, 32, 512), BF16),
            pltpu.VMEM((4, 256, 2048), BF16),
            pltpu.VMEM((2048, 256), BF16),
            pltpu.VMEM((2, 4, 4, 2, 2, 32, 256), BF16),
            pltpu.VMEM((2, 3, 4, 2, 2, 32, 256), BF16),
            pltpu.VMEM((2, 4, 2, 2, 32, 256), BF16),
            pltpu.VMEM((2, 3, 2, 2, 32, 256), BF16),
            pltpu.VMEM((2, 2, 2, 32, 256), BF16),
            pltpu.VMEM((2, 2, 32, 256), BF16),
            pltpu.VMEM((2, 4, 32, 256), BF16),
            pltpu.VMEM((2, 4, 4, 2, 32, 512), BF16),
            pltpu.VMEM((1024, 2048), BF16),
            pltpu.VMEM((512, 1024), F32),
            pltpu.SemaphoreType.DMA((84,)),
            pltpu.SemaphoreType.DMA((84,)),
            pltpu.SemaphoreType.DMA((9,)),
        ],
        compiler_params=pltpu.CompilerParams(
            collective_id=0, has_side_effects=True, vmem_limit_bytes=62 << 20
        ),
    )(
        features,
        w_trunk,
        w_head.reshape(4, 4, 2, 4, 32, 2048),
        bias_trunk.reshape(32, 128),
        bias_head.reshape(1, 2048),
        targets,
        block_mask,
    )


def solution(mesh):
    return jax.shard_map(
        body,
        mesh=mesh,
        in_specs=(
            P("cmp", "task"),
            P("task", "cmp"),
            P(None, "task"),
            P(),
            P("task"),
            P("cmp", "task"),
            P(),
        ),
        out_specs=(P("task", "cmp"), P("cmp", "task")),
        check_vma=False,
    )
```

time: 809 us -> 149 us (0.18)
  waiting for transfers between devices: 743 us -> 0 us
  Pallas kernels: 0 us -> 143 us
  matrix products: 40.2 us -> 0 us
  between operations: 14.2 us -> 0.65 us
    all_gather x5 -> x0, waiting for transfers between devices: 370 us -> none  [the longest x1 95.7 us: body(): lax.all_gather(jnp.where(pre_share > 0, grad_share, 0.0).astype(jnp.bfloa...]
    reduce_scatter x2 -> x0, waiting for transfers between devices: 208 us -> none  [the longest x1 169 us: body(): lax.psum_scatter(pre_part, 'task', scatter_dimension=1, tiled=True)]
    unnamed x9 -> x0, waiting for transfers between devices: 165 us -> none
    pallas_call x0 -> x1, Pallas kernels: none -> 143 us  [body(): pl.pallas_call(kernel, out_shape=(jax.ShapeDtypeStruct((512, 1024), F32),...]
    dot_general x6 -> x0, matrix products: 40.2 us -> none  [the longest x1 11.5 us: body(): jnp.dot(hidden, w_head, preferred_element_type=jnp.float32) + bias_head]
  transfers between devices with their start and end apart: 8 -> 0, of which waited for: 8 -> 0; matrix products, arithmetic and copies ran while one was open for 2% -> 0% of each run, Pallas kernels for 0% -> 0%
where the time goes in v1:
time: 149 us
  Pallas kernels  143 us (96%)
  local copies, waits for them, and re-layouts  5.33 us (4%)
    pallas_call x1, Pallas kernels, body(): pl.pallas_call(kernel, out_shape=(jax.ShapeDtypeStruct((512, 1024), F32),...  143 us
    unnamed x4, local copies, waits for them, and re-layouts  5.33 us

profile of v1, /device:TPU:1, one launch (start us, length us, event | category | flops | bytes accessed | tf_op | source)
XLA Modules:
  0.0 148.5 jit_solution(12396320669356705862)
XLA Ops:
  0.6 142.6 %shard_map.86 = (f32[512,1024]{1,0:T(8,128)}, bf16[1024,2048]{1,0:T(8,128)(2,1)}) custom-call(bf16[256,512]{1,0:T(8,128)(2,1)} %feat_hbm.1, bf16[512,1024]{1,0:T(8,128)(2,1)} %wt_hbm.1, bf16[4,4,2,4,32,2048]{5,4,3,2,1,0:T(8,128)(2,1)} %bitcast.3, f32[32,128]{1,0:T(8,128)} %bitcast.4, f32[1,2048]{1,0:T(1,128)} %bitcast.5, bf16[256,2048]{1,0:T(8,128)(2,1)} %tg_hbm.1, ...), custom_call_target="tpu_custom_call" | custom-call | tf_op jit(solution)/shard_map/pallas_call | solution.py:357
  143.2 0.0 copy-start
  143.2 3.3 %copy.11 = f32[512,1024]{1,0:T(8,128)} copy(f32[512,1024]{1,0:T(8,128)} %get-tuple-element.4) | data formatting | bytes 4194304
  146.5 0.0 copy-done
  146.5 2.0 %copy.12 = bf16[1024,2048]{1,0:T(8,128)(2,1)} copy(bf16[1024,2048]{1,0:T(8,128)(2,1)S(1)} %copy-done) | data formatting | bytes 8388608
Async XLA Ops:
  143.2 3.3 %copy-start = (bf16[1024,2048]{1,0:T(8,128)(2,1)S(1)}, bf16[1024,2048]{1,0:T(8,128)(2,1)}, u32[]{:S(2)}) copy-start(bf16[1024,2048]{1,0:T(8,128)(2,1)} %get-tuple-element.5) | copy-start | bytes 12582916

commit v2 on v0

v2 whole, which is shorter than its diff:
```python
import jax
import jax.numpy as jnp
from jax import lax
from jax.experimental import pallas as pl
from jax.experimental.pallas import tpu as pltpu
from jax.sharding import PartitionSpec as P

BLOCK = 512
MESH = pl.DeviceIdType.MESH
BF16 = jnp.bfloat16
F32 = jnp.float32
NEAR, FAR = (0, 1), (2, 3)
COPIES = 150
EARLY = 144


def dot(a, b):
    return jnp.dot(a, b, preferred_element_type=F32)


def dot_t(a, b):
    return lax.dot_general(a, b, (((1,), (1,)), ((), ())), preferred_element_type=F32)


def kernel(
    feat_hbm, wt_hbm, wh_hbm, bt_ref, bh_ref, tg_hbm, mask_ref,
    gt_hbm, gh_hbm,
    wh, wt, wtt, feat, featt, tg,
    p, p_in1, p_s1, p_in2, p_s2, p_in3, pre, pieces,
    h1, h1t, acc, h2n, h2f, gl, glt,
    q, q_in1, q_s1, q_in2, q_s2, q_in3, back, back_in, gpt,
    gh, gt, ssem, rsem, lsem,
):
    c = lax.axis_index("cmp")
    t = lax.axis_index("task")
    x, zh, y = t // 8, (t // 4) % 2, t % 4
    zl, core = c // 2, c % 2
    mate = 1 - core
    to_mate = {"cmp": 2 * zl + mate}
    to_twin = {"cmp": 2 * (1 - zl) + core}
    to_cross = {"cmp": 2 * (1 - zl) + mate}

    first, second = (x, y, x, y), (y, x, y, x)

    def to_first(k, d):
        if k % 2 == 0:
            return {"task": ((x + d) % 4) * 8 + zh * 4 + y}
        return {"task": x * 8 + zh * 4 + (y + d) % 4}

    def to_second(k, d):
        return to_first(k + 1, d)

    to_other_z = {"task": x * 8 + (1 - zh) * 4 + y}

    sent = []

    def send(src, dst, device):
        i = len(sent)
        copy = pltpu.make_async_remote_copy(
            src_ref=src, dst_ref=dst, send_sem=ssem.at[i], recv_sem=rsem.at[i],
            device_id=device, device_id_type=MESH,
        )
        copy.start()
        sent.append(copy)
        return copy

    local = []

    def fetch(src, dst):
        copy = pltpu.make_async_copy(src, dst, lsem.at[len(local)])
        copy.start()
        local.append(copy)
        return copy

    def wait_recv(copies):
        for copy in copies:
            copy.wait_recv()

    get_feat = fetch(feat_hbm, feat.at[core])
    get_wt = fetch(wt_hbm, wt)
    get_tg = fetch(tg_hbm, tg)
    get_wh = fetch(wh_hbm, wh)

    barrier = pltpu.get_barrier_semaphore()
    peers = [to_mate, to_twin, to_cross, to_other_z]
    peers += [to_first(k, d) for k in (0, 1) for d in (1, 2, 3)]
    for peer in peers:
        pl.semaphore_signal(barrier, inc=1, device_id=peer, device_id_type=MESH)
    pl.semaphore_wait(barrier, len(peers))

    get_feat.wait()
    f_twin = send(feat.at[core], feat.at[2 + core], to_twin)
    f_mate = send(feat.at[core], feat.at[core], to_mate)

    def turn_feat(slot):
        featt[slot] = feat[slot].T

    turn_feat(core)
    get_wt.wait()

    @pl.loop(0, 4)
    def _(i):
        block = wt[:, pl.ds(pl.multiple_of(i * 256, 256), 256)].T
        wtt[i] = block.reshape(2, 4, 32, 512)

    f_mate.wait_recv()
    turn_feat(mate)

    def start_sum(slots, tile, buf, arrive):
        copies = {k: [] for k in slots}
        for d in (2, 1, 3, 0):
            for k in slots:
                i = (first[k] + d) % 4
                tile(k, i)
                if d:
                    copies[k].append(send(buf.at[k, i], arrive.at[k, d - 1], to_first(k, d)))
        return copies

    def second_sum(slots, copies, buf, arrive, total, arrive2):
        out = {}
        for k in slots:
            wait_recv(copies[k])

            @pl.loop(0, 4)
            def _(j):
                for z in range(2):
                    value = buf[k, first[k], j, z].astype(F32)
                    for d in range(3):
                        value = value + arrive[k, d, j, z].astype(F32)
                    total[k, j, z] = value.astype(BF16)

            out[k] = [
                send(total.at[k, (second[k] + d) % 4], arrive2.at[k, d - 1], to_second(k, d))
                for d in (2, 1, 3)
            ]
        return out

    def third_sum(slots, copies, total, arrive2, total2, arrive3):
        out = {}
        for k in slots:
            wait_recv(copies[k])
            for z in range(2):
                value = total[k, second[k], z].astype(F32)
                for d in range(3):
                    value = value + arrive2[k, d, z].astype(F32)
                total2[k, z] = value.astype(BF16)
            out[k] = send(total2.at[k], arrive3.at[k], to_other_z)
        return out

    def last_sum(k, copies, total2, arrive3):
        copies[k].wait_recv()
        return [total2[k, z].astype(F32) + arrive3[k, z].astype(F32) for z in range(2)]

    def swap(slots, buf, dst):
        if slots == NEAR:
            return [send(buf.at[mate], dst(core), to_mate)]
        return [
            send(buf.at[2 + core], dst(2 + core), to_twin),
            send(buf.at[2 + mate], dst(2 + core), to_cross),
        ]

    def gather_small(slots, buf, base=0):
        out = {}
        for k in slots:
            part = buf.at[k - base, first[k], second[k]]
            out[k] = [send(part, part, to_second(k, d)) for d in (2, 1, 3)]
        return out

    def gather_large(slots, copies, buf, base=0):
        out = {}
        for k in slots:
            wait_recv(copies[k])
            part = buf.at[k - base, first[k]]
            out[k] = [send(part, part, to_first(k, d)) for d in (1, 3, 2)]
        return out

    def pre_tile(k, i):
        if k % 2 == 0:
            parts = [wtt[i, z, j] for j in range(4) for z in range(2)]
        else:
            parts = [wtt[j, z, i] for j in range(4) for z in range(2)]
        out = dot(jnp.concatenate(parts, axis=0), featt[k])
        p[k, i] = out.astype(BF16).reshape(4, 2, 32, 256)

    def pre_share(slots, copies):
        lane = lax.broadcasted_iota(jnp.int32, (32, 128), 1)
        unit = lax.broadcasted_iota(jnp.int32, (32, 128), 0)
        bias = []
        for z in range(2):
            row = jnp.broadcast_to(bt_ref[pl.ds(c * 8 + 2 * x + z, 1), :], (32, 128))
            column = jnp.where(lane == unit + y * 32, row, 0.0)
            bias.append(jnp.sum(column, axis=1, keepdims=True))
        for k in slots:
            sums = last_sum(k, copies, p_s2, p_in3)
            for z in range(2):
                value = sums[z] + bias[z]
                pre[k, z] = value
                value = jnp.maximum(value, 0.0).astype(BF16)
                pieces[k, z] = value
                if k in FAR:
                    h2f[k - 2, first[k], second[k], z] = value

    def place(parity):
        return x * (1 - parity) + y * parity, y * (1 - parity) + x * parity

    def hidden_slot(k):
        i, j = place(core)
        return h1.at[k, i, j]

    n1 = start_sum(NEAR, pre_tile, p, p_in1)
    f_twin.wait_recv()
    f_far = send(feat.at[2 + core], feat.at[2 + core], to_mate)
    turn_feat(2 + core)
    f_far.wait_recv()
    turn_feat(2 + mate)
    f1 = start_sum(FAR, pre_tile, p, p_in1)
    n2 = second_sum(NEAR, n1, p, p_in1, p_s1, p_in2)
    f2 = second_sum(FAR, f1, p, p_in1, p_s1, p_in2)
    n3 = third_sum(NEAR, n2, p_s1, p_in2, p_s2, p_in3)
    f3 = third_sum(FAR, f2, p_s1, p_in2, p_s2, p_in3)
    pre_share(NEAR, n3)
    n_swap = swap(NEAR, pieces, hidden_slot)
    i, j = place(core)
    for z in range(2):
        h1[core, i, j, z] = pieces[core, z]
    pre_share(FAR, f3)
    f_swap = swap(FAR, pieces, hidden_slot)
    wait_recv(n_swap)
    n_small = gather_small(NEAR, h1)
    wait_recv(f_swap)
    f_small = gather_small(FAR, h1)
    e_small = gather_small(FAR, h2f, 2)
    n_large = gather_large(NEAR, n_small, h1)
    f_large = gather_large(FAR, f_small, h1)

    def turn_hidden(k):
        @pl.loop(0, 4)
        def _(i):
            if k % 2 == 0:
                parts = [h1[k, i, j, z] for z in range(2) for j in range(4)]
            else:
                parts = [h1[k, j, i, z] for z in range(2) for j in range(4)]
            column = pl.multiple_of(k * 1024 + i * 256, 256)
            h1t[:, pl.ds(column, 256)] = jnp.concatenate(parts, axis=0).T

    for k in NEAR:
        wait_recv(n_large[k])
        turn_hidden(k)
    e_large = gather_large(FAR, e_small, h2f, 2)
    h_mate = send(h1.at[mate], h2n.at[core], to_mate)
    h_own = fetch(h1.at[core], h2n.at[core])
    get_wh.wait()

    @pl.loop(0, 4)
    def _(k):
        cols = pl.ds(pl.multiple_of(k * BLOCK, BLOCK), BLOCK)
        weight = wh[pl.ds(2 * zl, 2), :, :, :, :, cols].reshape(2048, BLOCK)
        acc[:, cols] = dot(h1t[:, :2048], weight)

    for k in FAR:
        wait_recv(f_large[k])
        turn_hidden(k)
    get_tg.wait()

    @pl.loop(0, 4)
    def _(k):
        cols = pl.ds(pl.multiple_of(k * BLOCK, BLOCK), BLOCK)
        weight = wh[pl.ds(2 - 2 * zl, 2), :, :, :, :, cols].reshape(2048, BLOCK)
        logits = acc[:, cols] + dot(h1t[:, 2048:], weight) + bh_ref[:, cols]
        seen = mask_ref[zl, t * 4 + k].astype(F32)
        error = seen * (jax.nn.sigmoid(logits) - tg[:, cols].astype(F32)) * (1.0 / 32.0)
        error = error.astype(BF16)
        gl[core, :, cols] = error
        glt[cols, :] = error.T

    parts = (pl.ds(0, EARLY), pl.ds(EARLY, 256 - EARLY))

    def send_errors(part):
        return send(gl.at[core, part], gl.at[2 + core, part], to_twin)

    g_early = send_errors(parts[0])
    g_mate = send(gl.at[core], gl.at[core], to_mate)

    def back_tile(k, i):
        quarter = 2 * (zl if k in NEAR else 1 - zl) + k % 2
        if k % 2 == 0:
            parts = [wh[quarter, i, z, j] for j in range(4) for z in range(2)]
        else:
            parts = [wh[quarter, j, z, i] for j in range(4) for z in range(2)]
        out = dot(jnp.concatenate(parts, axis=0), glt[...])
        q[k, i] = out.astype(BF16).reshape(4, 2, 32, 256)

    def back_share(slots, copies):
        for k in slots:
            sums = last_sum(k, copies, q_s2, q_in3)
            for z in range(2):
                back[k, z] = sums[z].astype(BF16)

    def back_slot(k):
        return back_in.at[k]

    def mask_share(slots):
        for k in slots:
            for z in range(2):
                value = jnp.where(pre[k, z] > 0.0, back_in[k, z].astype(F32), 0.0)
                gpt[k, first[k], second[k], z] = value.astype(BF16)

    n1 = start_sum(NEAR, back_tile, q, q_in1)
    f1 = start_sum(FAR, back_tile, q, q_in1)
    n2 = second_sum(NEAR, n1, q, q_in1, q_s1, q_in2)
    f2 = second_sum(FAR, f1, q, q_in1, q_s1, q_in2)
    n3 = third_sum(NEAR, n2, q_s1, q_in2, q_s2, q_in3)
    f3 = third_sum(FAR, f2, q_s1, q_in2, q_s2, q_in3)
    back_share(NEAR, n3)
    n_swap = swap(NEAR, back, back_slot)
    for z in range(2):
        back_in[core, z] = back[core, z]
    back_share(FAR, f3)
    f_swap = swap(FAR, back, back_slot)
    g_late = send_errors(parts[1])
    wait_recv(n_swap)
    mask_share(NEAR)
    n_small = gather_small(NEAR, gpt)
    wait_recv(f_swap)
    mask_share(FAR)
    f_small = gather_small(FAR, gpt)
    n_large = gather_large(NEAR, n_small, gpt)
    f_large = gather_large(FAR, f_small, gpt)

    g_far = []
    for copy, part in zip((g_early, g_late), parts):
        copy.wait_recv()
        g_far.append(send(gl.at[2 + core, part], gl.at[2 + core, part], to_mate))
    h_own.wait()
    h_mate.wait_recv()
    for k in FAR:
        wait_recv(e_large[k])
    g_mate.wait_recv()
    wait_recv(g_far)

    def chain_tile(buf, k, i, parity):
        parts = []
        for z in range(2):
            for j in range(4):
                a, b = i * (1 - parity) + j * parity, j * (1 - parity) + i * parity
                parts.append(buf[k, a, b, z])
        return jnp.concatenate(parts, axis=0)

    for i in range(4):
        tile = [chain_tile(h2n, k, i, core) for k in NEAR]
        tile += [chain_tile(h2f, k - 2, i, k % 2) for k in FAR]
        tile = jnp.concatenate(tile, axis=1)

        @pl.loop(0, 4)
        def _(k):
            cols = pl.ds(pl.multiple_of(k * 512, 512), 512)
            out = dot(tile, gl[:, :, cols].reshape(1024, 512))
            gh[pl.ds(i * 256, 256), cols] = out.astype(BF16)

        fetch(gh.at[pl.ds(i * 256, 256)], gh_hbm.at[pl.ds(i * 256, 256)])

    for k in NEAR:
        wait_recv(n_large[k])
    for i in range(4):
        out = sum(dot_t(featt[k], chain_tile(gpt, k, i, k % 2)) for k in NEAR)
        gt[:, i * 256 : (i + 1) * 256] = out
    for k in FAR:
        wait_recv(f_large[k])
    for i in range(4):
        out = sum(dot_t(featt[k], chain_tile(gpt, k, i, k % 2)) for k in FAR)
        gt[:, i * 256 : (i + 1) * 256] += out
    fetch(gt, gt_hbm)
    for copy in local[5:]:
        copy.wait()
    for copy in sent:
        copy.wait_send()


def copy_kernel(gt_in, gh_in, gt_out, gh_out, gt, gh, sem):
    ins, outs = [], []
    for src, mid, dst in ((gt_in, gt, gt_out), (gh_in, gh, gh_out)):
        rows = src.shape[0] // 4
        for i in range(4):
            part = pl.ds(i * rows, rows)
            n = len(ins)
            ins.append(pltpu.make_async_copy(src.at[part], mid.at[part], sem.at[0, n]))
            outs.append(pltpu.make_async_copy(mid.at[part], dst.at[part], sem.at[1, n]))
    for copy in ins:
        copy.start()
    for copy, out in zip(ins, outs):
        copy.wait()
        out.start()
    for out in outs:
        out.wait()


def body(features, w_trunk, w_head, bias_trunk, bias_head, targets, block_mask):
    hbm = pl.BlockSpec(memory_space=pl.ANY)
    vmem = pl.BlockSpec(memory_space=pltpu.VMEM)
    outs = (
        jax.ShapeDtypeStruct((512, 1024), F32),
        jax.ShapeDtypeStruct((1024, 2048), BF16),
    )
    chain = (4, 4, 2, 32, 256)
    results = pl.pallas_call(
        kernel,
        out_shape=outs,
        in_specs=[hbm, hbm, hbm, vmem, vmem, hbm, pl.BlockSpec(memory_space=pltpu.SMEM)],
        out_specs=(hbm, hbm),
        scratch_shapes=[
            pltpu.VMEM((4, 4, 2, 4, 32, 2048), BF16),
            pltpu.VMEM((512, 1024), BF16),
            pltpu.VMEM((4, 2, 4, 32, 512), BF16),
            pltpu.VMEM((4, 256, 512), BF16),
            pltpu.VMEM((4, 512, 256), BF16),
            pltpu.VMEM((256, 2048), BF16),
            pltpu.VMEM((4, *chain), BF16),
            pltpu.VMEM((4, 3, 4, 2, 32, 256), BF16),
            pltpu.VMEM((4, 4, 2, 32, 256), BF16),
            pltpu.VMEM((4, 3, 2, 32, 256), BF16),
            pltpu.VMEM((4, 2, 32, 256), BF16),
            pltpu.VMEM((4, 2, 32, 256), BF16),
            pltpu.VMEM((4, 2, 32, 256), F32),
            pltpu.VMEM((4, 2, 32, 256), BF16),
            pltpu.VMEM((4, *chain), BF16),
            pltpu.VMEM((256, 4096), BF16),
            pltpu.VMEM((256, 2048), F32),
            pltpu.VMEM((2, *chain), BF16),
            pltpu.VMEM((2, *chain), BF16),
            pltpu.VMEM((4, 256, 2048), BF16),
            pltpu.VMEM((2048, 256), BF16),
            pltpu.VMEM((4, *chain), BF16),
            pltpu.VMEM((4, 3, 4, 2, 32, 256), BF16),
            pltpu.VMEM((4, 4, 2, 32, 256), BF16),
            pltpu.VMEM((4, 3, 2, 32, 256), BF16),
            pltpu.VMEM((4, 2, 32, 256), BF16),
            pltpu.VMEM((4, 2, 32, 256), BF16),
            pltpu.VMEM((4, 2, 32, 256), BF16),
            pltpu.VMEM((4, 2, 32, 256), BF16),
            pltpu.VMEM((4, *chain), BF16),
            pltpu.VMEM((1024, 2048), BF16),
            pltpu.VMEM((512, 1024), F32),
            pltpu.SemaphoreType.DMA((COPIES,)),
            pltpu.SemaphoreType.DMA((COPIES,)),
            pltpu.SemaphoreType.DMA((10,)),
        ],
        compiler_params=pltpu.CompilerParams(
            collective_id=0, has_side_effects=True, vmem_limit_bytes=62 << 20
        ),
    )(
        features,
        w_trunk,
        w_head.reshape(4, 4, 2, 4, 32, 2048),
        bias_trunk.reshape(32, 128),
        bias_head.reshape(1, 2048),
        targets,
        block_mask,
    )
    return pl.pallas_call(
        copy_kernel,
        out_shape=outs,
        in_specs=[hbm, hbm],
        out_specs=(hbm, hbm),
        scratch_shapes=[
            pltpu.VMEM((512, 1024), F32),
            pltpu.VMEM((1024, 2048), BF16),
            pltpu.SemaphoreType.DMA((2, 8)),
        ],
        compiler_params=pltpu.CompilerParams(vmem_limit_bytes=60 << 20),
    )(*results)


def solution(mesh):
    return jax.shard_map(
        body,
        mesh=mesh,
        in_specs=(
            P("cmp", "task"),
            P("task", "cmp"),
            P(None, "task"),
            P(),
            P("task"),
            P("cmp", "task"),
            P(),
        ),
        out_specs=(P("task", "cmp"), P("cmp", "task")),
        check_vma=False,
    )
```

time: 809 us -> 113 us (0.14)
  waiting for transfers between devices: 743 us -> 0 us
  Pallas kernels: 0 us -> 112 us
  matrix products: 40.2 us -> 0 us
  between operations: 14.2 us -> 0.64 us
    all_gather x5 -> x0, waiting for transfers between devices: 370 us -> none  [the longest x1 95.7 us: body(): lax.all_gather(jnp.where(pre_share > 0, grad_share, 0.0).astype(jnp.bfloa...]
    reduce_scatter x2 -> x0, waiting for transfers between devices: 208 us -> none  [the longest x1 169 us: body(): lax.psum_scatter(pre_part, 'task', scatter_dimension=1, tiled=True)]
    unnamed x9 -> x0, waiting for transfers between devices: 165 us -> none
    pallas_call x0 -> x2, Pallas kernels: none -> 112 us  [the longest x1 106 us: body(): pl.pallas_call(kernel, out_shape=outs, in_specs=[hbm, hbm, hbm, vmem, vme...]
    dot_general x6 -> x0, matrix products: 40.2 us -> none  [the longest x1 11.5 us: body(): jnp.dot(hidden, w_head, preferred_element_type=jnp.float32) + bias_head]
  transfers between devices with their start and end apart: 8 -> 0, of which waited for: 8 -> 0; matrix products, arithmetic and copies ran while one was open for 2% -> 0% of each run, Pallas kernels for 0% -> 0%
where the time goes in v2:
time: 113 us; the launch traced here: 112 us
  Pallas kernels  112 us (99%)
    pallas_call x1, Pallas kernels, body(): pl.pallas_call(kernel, out_shape=outs, in_specs=[hbm, hbm, hbm, vmem, vme...  106 us
    pallas_call x1, Pallas kernels, body(): pl.pallas_call(copy_kernel, out_shape=outs, in_specs=[hbm, hbm], out_spec...  5.43 us

profile of v2, /device:TPU:1, one launch (start us, length us, event | category | flops | bytes accessed | tf_op | source)
XLA Modules:
  0.0 112.5 jit_solution(14008869165646709119)
XLA Ops:
  0.6 106.4 %shard_map.86 = (f32[512,1024]{1,0:T(8,128)}, bf16[1024,2048]{1,0:T(8,128)(2,1)}) custom-call(bf16[256,512]{1,0:T(8,128)(2,1)} %feat_hbm.1, bf16[512,1024]{1,0:T(8,128)(2,1)} %wt_hbm.1, bf16[4,4,2,4,32,2048]{5,4,3,2,1,0:T(8,128)(2,1)} %bitcast.3, f32[32,128]{1,0:T(8,128)} %bitcast.4, f32[1,2048]{1,0:T(1,128)} %bitcast.5, bf16[256,2048]{1,0:T(8,128)(2,1)} %tg_hbm.1, ...), custom_call_target="tpu_custom_call" | custom-call | tf_op jit(solution)/shard_map/pallas_call | solution.py:405
  107.0 5.4 %shard_map.87 = (f32[512,1024]{1,0:T(8,128)}, bf16[1024,2048]{1,0:T(8,128)(2,1)}) custom-call(f32[512,1024]{1,0:T(8,128)} %get-tuple-element.4.gt_in, bf16[1024,2048]{1,0:T(8,128)(2,1)} %get-tuple-element.5.gh_in), custom_call_target="tpu_custom_call" | custom-call | tf_op jit(solution)/shard_map/pallas_call | solution.py:459

commit v3 on v0

v3 whole, which is shorter than its diff:
```python
import jax
import jax.numpy as jnp
from jax import lax
from jax.experimental import pallas as pl
from jax.experimental.pallas import tpu as pltpu
from jax.sharding import PartitionSpec as P

BLOCK = 512
MESH = pl.DeviceIdType.MESH
BF16 = jnp.bfloat16
F32 = jnp.float32
NEAR, FAR, ALL = (0, 1), (2, 3), (0, 1, 2, 3)
HALF = 128
COPIES = 272


def dot(a, b):
    return jnp.dot(a, b, preferred_element_type=F32)


def dot_t(a, b):
    return lax.dot_general(a, b, (((1,), (1,)), ((), ())), preferred_element_type=F32)


def kernel(
    feat_hbm, wt_hbm, wh_hbm, bt_ref, bh_ref, tg_hbm, mask_ref,
    gt_hbm, gh_hbm,
    wh, wt, wtt, feat, featt, tg,
    p, p_in1, p_s1, p_in2, p_s2, p_in3, p_far, pre, pieces,
    h1, h1t, h2n, h2f, gl, glt,
    q, q_in1, q_s1, q_in2, q_s2, q_in3, q_far, back, back_in, gpt,
    gh, gt, ssem, rsem, lsem,
):
    c = lax.axis_index("cmp")
    t = lax.axis_index("task")
    x, zh, y = t // 8, (t // 4) % 2, t % 4
    zl, core = c // 2, c % 2
    mate = 1 - core
    to_mate = {"cmp": 2 * zl + mate}
    to_twin = {"cmp": 2 * (1 - zl) + core}
    to_cross = {"cmp": 2 * (1 - zl) + mate}

    first, second = (x, y, x, y), (y, x, y, x)

    def to_first(k, d):
        if k % 2 == 0:
            return {"task": ((x + d) % 4) * 8 + zh * 4 + y}
        return {"task": x * 8 + zh * 4 + (y + d) % 4}

    def to_second(k, d):
        return to_first(k + 1, d)

    other_z = x * 8 + (1 - zh) * 4 + y
    to_other_z = {"task": other_z}
    to_far = (
        (2 + core, to_twin), (2 + core, {**to_twin, "task": other_z}),
        (2 + mate, to_cross), (2 + mate, {**to_cross, "task": other_z}),
    )

    sent = []

    def send(src, dst, device):
        i = len(sent)
        copy = pltpu.make_async_remote_copy(
            src_ref=src, dst_ref=dst, send_sem=ssem.at[i], recv_sem=rsem.at[i],
            device_id=device, device_id_type=MESH,
        )
        copy.start()
        sent.append(copy)
        return copy

    local = []

    def fetch(src, dst):
        copy = pltpu.make_async_copy(src, dst, lsem.at[len(local)])
        copy.start()
        local.append(copy)
        return copy

    def wait_recv(copies):
        for copy in copies:
            copy.wait_recv()

    get_feat = fetch(feat_hbm, feat.at[core])
    get_wt = fetch(wt_hbm, wt)
    get_tg = fetch(tg_hbm, tg)
    get_wh = fetch(wh_hbm, wh)

    barrier = pltpu.get_barrier_semaphore()
    peers = [to_mate, to_other_z] + [device for _, device in to_far]
    peers += [to_first(k, d) for k in (0, 1) for d in (1, 2, 3)]
    for peer in peers:
        pl.semaphore_signal(barrier, inc=1, device_id=peer, device_id_type=MESH)
    pl.semaphore_wait(barrier, len(peers))

    get_feat.wait()
    halves = [slice(w * HALF, (w + 1) * HALF) for w in range(2)]
    f_twin = [send(feat.at[core, rows], feat.at[2 + core, rows], to_twin) for rows in halves]
    f_mate = send(feat.at[core], feat.at[core], to_mate)

    def turn_feat(slot, rows):
        featt[slot, :, rows] = feat[slot, rows, :].T

    for rows in halves:
        turn_feat(core, rows)
    get_wt.wait()

    @pl.loop(0, 4)
    def _(i):
        block = wt[:, pl.ds(pl.multiple_of(i * 256, 256), 256)].T
        wtt[i] = block.reshape(2, 4, 32, 512)

    f_mate.wait_recv()
    for rows in halves:
        turn_feat(mate, rows)

    def start_sum(slots, tile, buf, arrive, steps=(2, 1, 3, 0)):
        copies = {k: [] for k in slots}
        for d in steps:
            for k in slots:
                i = (first[k] + d) % 4
                tile(k, i)
                if d:
                    copies[k].append(send(buf.at[k, i], arrive.at[k, d - 1], to_first(k, d)))
        return copies

    def second_sum(slots, copies, buf, arrive, total, arrive2):
        out = {}
        for k in slots:
            wait_recv(copies[k])

            @pl.loop(0, 4)
            def _(j):
                for z in range(2):
                    value = buf[k, first[k], j, z].astype(F32)
                    for d in range(3):
                        value = value + arrive[k, d, j, z].astype(F32)
                    total[k, j, z] = value.astype(BF16)

            out[k] = [
                send(total.at[k, (second[k] + d) % 4], arrive2.at[k, d - 1], to_second(k, d))
                for d in (2, 1, 3)
            ]
        return out

    def end_second(slots, copies, total, arrive2, total2):
        for k in slots:
            wait_recv(copies[k])
            for z in range(2):
                value = total[k, second[k], z].astype(F32)
                for d in range(3):
                    value = value + arrive2[k, d, z].astype(F32)
                total2[k, z] = value.astype(BF16)

    def third_sum(slots, total2, arrive3):
        return {k: send(total2.at[k], arrive3.at[k], to_other_z) for k in slots}

    def last_sum(k, copies, total2, arrive3):
        copies[k].wait_recv()
        return [total2[k, z].astype(F32) + arrive3[k, z].astype(F32) for z in range(2)]

    def swap_near(buf, dst):
        return [send(buf.at[mate], dst(core), to_mate)]

    def swap_far(total2, dst):
        return [send(total2.at[k], dst.at[core, zh], device) for k, device in to_far]

    def gather_small(slots, buf, base=0):
        out = {}
        for k in slots:
            part = buf.at[k - base, first[k], second[k]]
            out[k] = [send(part, part, to_second(k, d)) for d in (2, 1, 3)]
        return out

    def gather_large(slots, copies, buf, base=0, steps=(2, 1, 3)):
        out = {}
        for k in slots:
            wait_recv(copies[k])
            out[k] = more_large(k, buf, base, steps)
        return out

    def more_large(k, buf, base, steps):
        part = buf.at[k - base, first[k]]
        return [send(part, part, to_first(k, d)) for d in steps]

    class Wave:
        def __init__(self, bufs, tile, share, buf, dst, far_in, own, place_share, gathered):
            self.parts, self.in1, self.s1, self.in2, self.s2, self.in3 = bufs
            self.tile, self.share, self.buf, self.dst = tile, share, buf, dst
            self.far_in, self.own, self.place_share, self.gathered = far_in, own, place_share, gathered
            self.first = {}

        def sum_first(self, slots):
            self.first.update(start_sum(slots, self.tile, self.parts, self.in1))

        def sum_second(self):
            self.second = second_sum(ALL, self.first, self.parts, self.in1, self.s1, self.in2)

        def sum_third(self):
            end_second(NEAR, self.second, self.s1, self.in2, self.s2)
            self.third = third_sum(NEAR, self.s2, self.in3)
            end_second(FAR, self.second, self.s1, self.in2, self.s2)
            self.far = swap_far(self.s2, self.far_in)

        def third_far(self):
            return third_sum(FAR, self.s2, self.in3)

        def gather_second(self):
            self.share(NEAR, self.third)
            near = swap_near(self.buf, self.dst)
            self.own()
            wait_recv(self.far)
            self.place_share(FAR)
            wait_recv(near)
            self.place_share(NEAR)
            self.small = gather_small(ALL, self.gathered)

        def gather_first(self):
            self.large = gather_large(ALL, self.small, self.gathered)

        def wait(self):
            for k in ALL:
                wait_recv(self.large[k])

    def pre_wave(w):
        parts, in1, s1, in2, s2, in3, from_far, mine, piece, hidden, hidden_far = (
            buf.at[w] for buf in (p, p_in1, p_s1, p_in2, p_s2, p_in3, p_far, pre, pieces, h1, h2f)
        )
        lanes = slice(w * HALF, (w + 1) * HALF)

        def tile(k, i):
            if k % 2 == 0:
                rows = [wtt[i, z, j] for j in range(4) for z in range(2)]
            else:
                rows = [wtt[j, z, i] for j in range(4) for z in range(2)]
            out = dot(jnp.concatenate(rows, axis=0), featt[k, :, lanes])
            parts[k, i] = out.astype(BF16).reshape(4, 2, 32, HALF)

        def share(slots, copies):
            for k in slots:
                sums = last_sum(k, copies, s2, in3)
                for z in range(2):
                    value = sums[z] + bias(c, z)
                    mine[k, z] = value
                    value = jnp.maximum(value, 0.0).astype(BF16)
                    piece[k, z] = value
                    if k in FAR:
                        hidden_far[k - 2, first[k], second[k], z] = value

        def own():
            i, j = place(core)
            for z in range(2):
                hidden[core, i, j, z] = piece[core, z]

        def slot(k):
            i, j = place(core)
            return hidden.at[k, i, j]

        def place_hidden(slots):
            if slots == NEAR:
                return
            for k in FAR:
                for z in range(2):
                    value = from_far[k - 2, 0, z].astype(F32) + from_far[k - 2, 1, z].astype(F32)
                    value = jnp.maximum(value + bias(2 - 2 * zl + k % 2, z), 0.0)
                    hidden[k, first[k], second[k], z] = value.astype(BF16)

        return Wave((parts, in1, s1, in2, s2, in3), tile, share, piece, slot, from_far, own, place_hidden, hidden)

    def bias(quarter, z):
        lane = lax.broadcasted_iota(jnp.int32, (32, 128), 1)
        unit = lax.broadcasted_iota(jnp.int32, (32, 128), 0)
        row = jnp.broadcast_to(bt_ref[pl.ds(quarter * 8 + 2 * x + z, 1), :], (32, 128))
        return jnp.sum(jnp.where(lane == unit + y * 32, row, 0.0), axis=1, keepdims=True)

    def place(parity):
        return x * (1 - parity) + y * parity, y * (1 - parity) + x * parity

    waves = [pre_wave(w) for w in range(2)]
    for wave in waves:
        wave.sum_first(NEAR)
    for wave, copy, rows in zip(waves, f_twin, halves):
        copy.wait_recv()
        f_far = send(feat.at[2 + core, rows], feat.at[2 + core, rows], to_mate)
        turn_feat(2 + core, rows)
        f_far.wait_recv()
        turn_feat(2 + mate, rows)
        wave.sum_first(FAR)
    for wave in waves:
        wave.sum_second()
    for wave in waves:
        wave.sum_third()
    own_far = [wave.third_far() for wave in waves]
    for wave in waves:
        wave.gather_second()
    for wave in waves:
        wave.gather_first()
    e_small = []
    for w in range(2):
        waves[w].share(FAR, own_far[w])
        e_small.append(gather_small(FAR, h2f.at[w], 2))

    def turn_hidden(w):
        for k in ALL:
            @pl.loop(0, 4)
            def _(i):
                if k % 2 == 0:
                    parts = [h1[w, k, i, j, z] for z in range(2) for j in range(4)]
                else:
                    parts = [h1[w, k, j, i, z] for z in range(2) for j in range(4)]
                quarter = 2 * (zl if k in NEAR else 1 - zl) + k % 2
                column = pl.multiple_of(quarter * 1024 + i * 256, 256)
                h1t[w, :, pl.ds(column, 256)] = jnp.concatenate(parts, axis=0).T

    def logit_errors(w):
        rows = slice(w * HALF, (w + 1) * HALF)

        @pl.loop(0, 4)
        def _(k):
            cols = pl.ds(pl.multiple_of(k * BLOCK, BLOCK), BLOCK)
            weight = wh[:, :, :, :, :, cols].reshape(4096, BLOCK)
            logits = dot(h1t[w], weight) + bh_ref[:, cols]
            chance = 0.5 + 0.5 * jnp.tanh(0.5 * logits)
            seen = mask_ref[zl, t * 4 + k].astype(F32)
            error = seen * (chance - tg[rows, cols].astype(F32)) * (1.0 / 32.0)
            error = error.astype(BF16)
            gl[core, rows, cols] = error
            glt[w, cols, :] = error.T

    def back_wave(w):
        parts, in1, s1, in2, s2, in3, from_far, mine, piece, piece_in, grad = (
            buf.at[w] for buf in (q, q_in1, q_s1, q_in2, q_s2, q_in3, q_far, pre, back, back_in, gpt)
        )

        def tile(k, i):
            quarter = 2 * (zl if k in NEAR else 1 - zl) + k % 2
            if k % 2 == 0:
                rows = [wh[quarter, i, z, j] for j in range(4) for z in range(2)]
            else:
                rows = [wh[quarter, j, z, i] for j in range(4) for z in range(2)]
            out = dot(jnp.concatenate(rows, axis=0), glt[w])
            parts[k, i] = out.astype(BF16).reshape(4, 2, 32, HALF)

        def share(slots, copies):
            for k in slots:
                sums = last_sum(k, copies, s2, in3)
                for z in range(2):
                    piece[k, z] = sums[z].astype(BF16)

        def own():
            for z in range(2):
                piece_in[core, z] = piece[core, z]

        def slot(k):
            return piece_in.at[k]

        def mask_share(slots):
            for k in slots:
                for z in range(2):
                    if k in NEAR:
                        value = piece_in[k, z].astype(F32)
                    else:
                        value = from_far[k - 2, 0, z].astype(F32) + from_far[k - 2, 1, z].astype(F32)
                    value = jnp.where(mine[k, z] > 0.0, value, 0.0)
                    grad[k, first[k], second[k], z] = value.astype(BF16)

        return Wave((parts, in1, s1, in2, s2, in3), tile, share, piece, slot, from_far, own, mask_share, grad)

    g_rows, g_twin = [], []

    def send_errors(start, count):
        part = pl.ds(start, count)
        g_rows.append(part)
        g_twin.append(send(gl.at[core, part], gl.at[2 + core, part], to_twin))

    backs = [back_wave(w) for w in range(2)]
    e_large, h_mate, h_own, g_mate = [], [], [], []
    for w in range(2):
        waves[w].wait()
        turn_hidden(w)
        if w == 0:
            get_wh.wait()
            get_tg.wait()
        logit_errors(w)
        if w == 0:
            send_errors(0, HALF)
        else:
            send_errors(HALF, 48)
            backs[0].sum_second()
        backs[w].sum_first(ALL)
        h_mate.append(send(h1.at[w, mate], h2n.at[w, core], to_mate))
        h_own.append(fetch(h1.at[w, core], h2n.at[w, core]))
        part = pl.ds(w * HALF, HALF)
        g_mate.append(send(gl.at[core, part], gl.at[core, part], to_mate))
        if w == 0:
            e_large = [gather_large(FAR, e_small[v], h2f.at[v], 2) for v in range(2)]
    backs[0].sum_third()
    send_errors(HALF + 48, 64)
    backs[1].sum_second()
    backs[1].sum_third()
    send_errors(HALF + 112, 16)
    for wave in backs:
        wave.gather_second()
    for wave in backs:
        wave.gather_first()

    g_far = []
    for copy, part in zip(g_twin, g_rows):
        copy.wait_recv()
        g_far.append(send(gl.at[2 + core, part], gl.at[2 + core, part], to_mate))
    for copy in h_own:
        copy.wait()
    wait_recv(h_mate)
    for copies in e_large:
        for k in FAR:
            wait_recv(copies[k])
    wait_recv(g_mate)
    wait_recv(g_far)

    def chain_tile(buf, k, i, parity):
        parts = []
        for z in range(2):
            for j in range(4):
                a, b = i * (1 - parity) + j * parity, j * (1 - parity) + i * parity
                parts.append(buf[k, a, b, z])
        return jnp.concatenate(parts, axis=0)

    for i in range(4):
        tile = [chain_tile(h2n.at[w], k, i, core) for k in NEAR for w in range(2)]
        tile += [chain_tile(h2f.at[w], k - 2, i, k % 2) for k in FAR for w in range(2)]
        tile = jnp.concatenate(tile, axis=1)

        @pl.loop(0, 4)
        def _(k):
            cols = pl.ds(pl.multiple_of(k * 512, 512), 512)
            out = dot(tile, gl[:, :, cols].reshape(1024, 512))
            gh[pl.ds(i * 256, 256), cols] = out.astype(BF16)

        fetch(gh.at[pl.ds(i * 256, 256)], gh_hbm.at[pl.ds(i * 256, 256)])

    for w in range(2):
        backs[w].wait()
        known = jnp.concatenate([featt[k, :, w * HALF : (w + 1) * HALF] for k in ALL], axis=1)
        for i in range(4):
            cols = slice(i * 256, (i + 1) * 256)
            grad = jnp.concatenate([chain_tile(gpt.at[w], k, i, k % 2) for k in ALL], axis=1)
            if w == 0:
                gt[:, cols] = dot_t(known, grad)
            else:
                gt[:, cols] += dot_t(known, grad)
    fetch(gt, gt_hbm)
    for copy in local[6:]:
        copy.wait()
    for copy in sent:
        copy.wait_send()


def body(features, w_trunk, w_head, bias_trunk, bias_head, targets, block_mask):
    hbm = pl.BlockSpec(memory_space=pl.ANY)
    vmem = pl.BlockSpec(memory_space=pltpu.VMEM)
    outs = (
        jax.ShapeDtypeStruct((512, 1024), F32),
        jax.ShapeDtypeStruct((1024, 2048), BF16),
    )
    chain = (4, 4, 2, 32, HALF)
    return pl.pallas_call(
        kernel,
        out_shape=outs,
        in_specs=[hbm, hbm, hbm, vmem, vmem, hbm, pl.BlockSpec(memory_space=pltpu.SMEM)],
        out_specs=(hbm, hbm),
        scratch_shapes=[
            pltpu.VMEM((4, 4, 2, 4, 32, 2048), BF16),
            pltpu.VMEM((512, 1024), BF16),
            pltpu.VMEM((4, 2, 4, 32, 512), BF16),
            pltpu.VMEM((4, 256, 512), BF16),
            pltpu.VMEM((4, 512, 256), BF16),
            pltpu.VMEM((256, 2048), BF16),
            pltpu.VMEM((2, 4, *chain), BF16),
            pltpu.VMEM((2, 4, 3, 4, 2, 32, HALF), BF16),
            pltpu.VMEM((2, 4, 4, 2, 32, HALF), BF16),
            pltpu.VMEM((2, 4, 3, 2, 32, HALF), BF16),
            pltpu.VMEM((2, 4, 2, 32, HALF), BF16),
            pltpu.VMEM((2, 4, 2, 32, HALF), BF16),
            pltpu.VMEM((2, 2, 2, 2, 32, HALF), BF16),
            pltpu.VMEM((2, 4, 2, 32, HALF), F32),
            pltpu.VMEM((2, 4, 2, 32, HALF), BF16),
            pltpu.VMEM((2, 4, *chain), BF16),
            pltpu.VMEM((2, HALF, 4096), BF16),
            pltpu.VMEM((2, 2, *chain), BF16),
            pltpu.VMEM((2, 2, *chain), BF16),
            pltpu.VMEM((4, 256, 2048), BF16),
            pltpu.VMEM((2, 2048, HALF), BF16),
            pltpu.VMEM((2, 4, *chain), BF16),
            pltpu.VMEM((2, 4, 3, 4, 2, 32, HALF), BF16),
            pltpu.VMEM((2, 4, 4, 2, 32, HALF), BF16),
            pltpu.VMEM((2, 4, 3, 2, 32, HALF), BF16),
            pltpu.VMEM((2, 4, 2, 32, HALF), BF16),
            pltpu.VMEM((2, 4, 2, 32, HALF), BF16),
            pltpu.VMEM((2, 2, 2, 2, 32, HALF), BF16),
            pltpu.VMEM((2, 4, 2, 32, HALF), BF16),
            pltpu.VMEM((2, 4, 2, 32, HALF), BF16),
            pltpu.VMEM((2, 4, *chain), BF16),
            pltpu.VMEM((1024, 2048), BF16),
            pltpu.VMEM((512, 1024), F32),
            pltpu.SemaphoreType.DMA((COPIES,)),
            pltpu.SemaphoreType.DMA((COPIES,)),
            pltpu.SemaphoreType.DMA((11,)),
        ],
        compiler_params=pltpu.CompilerParams(
            collective_id=0, has_side_effects=True, vmem_limit_bytes=62 << 20
        ),
    )(
        features,
        w_trunk,
        w_head.reshape(4, 4, 2, 4, 32, 2048),
        bias_trunk.reshape(32, 128),
        bias_head.reshape(1, 2048),
        targets,
        block_mask,
    )


def solution(mesh):
    return jax.shard_map(
        body,
        mesh=mesh,
        in_specs=(
            P("cmp", "task"),
            P("task", "cmp"),
            P(None, "task"),
            P(),
            P("task"),
            P("cmp", "task"),
            P(),
        ),
        out_specs=(P("task", "cmp"), P("cmp", "task")),
        check_vma=False,
    )
```

time: 809 us -> 105 us (0.13)
  waiting for transfers between devices: 743 us -> 0 us
  Pallas kernels: 0 us -> 99.1 us
  matrix products: 40.2 us -> 0 us
  between operations: 14.2 us -> 0.65 us
    all_gather x5 -> x0, waiting for transfers between devices: 370 us -> none  [the longest x1 95.7 us: body(): lax.all_gather(jnp.where(pre_share > 0, grad_share, 0.0).astype(jnp.bfloa...]
    reduce_scatter x2 -> x0, waiting for transfers between devices: 208 us -> none  [the longest x1 169 us: body(): lax.psum_scatter(pre_part, 'task', scatter_dimension=1, tiled=True)]
    unnamed x9 -> x0, waiting for transfers between devices: 165 us -> none
    pallas_call x0 -> x1, Pallas kernels: none -> 99.1 us  [body(): pl.pallas_call(kernel, out_shape=outs, in_specs=[hbm, hbm, hbm, vmem, vme...]
    dot_general x6 -> x0, matrix products: 40.2 us -> none  [the longest x1 11.5 us: body(): jnp.dot(hidden, w_head, preferred_element_type=jnp.float32) + bias_head]
  transfers between devices with their start and end apart: 8 -> 0, of which waited for: 8 -> 0; matrix products, arithmetic and copies ran while one was open for 2% -> 0% of each run, Pallas kernels for 0% -> 0%
where the time goes in v3:
time: 105 us
  Pallas kernels  99.1 us (94%)
  local copies, waits for them, and re-layouts  5.33 us (5%)
    pallas_call x1, Pallas kernels, body(): pl.pallas_call(kernel, out_shape=outs, in_specs=[hbm, hbm, hbm, vmem, vme...  99.1 us
    unnamed x4, local copies, waits for them, and re-layouts  5.33 us

profile of v3, /device:TPU:1, one launch (start us, length us, event | category | flops | bytes accessed | tf_op | source)
XLA Modules:
  0.0 105.1 jit_solution(4814600686428376556)
XLA Ops:
  0.6 99.1 %shard_map.86 = (f32[512,1024]{1,0:T(8,128)}, bf16[1024,2048]{1,0:T(8,128)(2,1)}) custom-call(bf16[256,512]{1,0:T(8,128)(2,1)} %feat_hbm.1, bf16[512,1024]{1,0:T(8,128)(2,1)} %wt_hbm.1, bf16[4,4,2,4,32,2048]{5,4,3,2,1,0:T(8,128)(2,1)} %bitcast.3, f32[32,128]{1,0:T(8,128)} %bitcast.4, f32[1,2048]{1,0:T(1,128)} %bitcast.5, bf16[256,2048]{1,0:T(8,128)(2,1)} %tg_hbm.1, ...), custom_call_target="tpu_custom_call" | custom-call | tf_op jit(solution)/shard_map/pallas_call | solution.py:466
  99.8 0.0 copy-start
  99.8 3.3 %copy.11 = f32[512,1024]{1,0:T(8,128)} copy(f32[512,1024]{1,0:T(8,128)} %get-tuple-element.4) | data formatting | bytes 4194304
  103.1 0.0 copy-done
  103.1 2.0 %copy.12 = bf16[1024,2048]{1,0:T(8,128)(2,1)} copy(bf16[1024,2048]{1,0:T(8,128)(2,1)S(1)} %copy-done) | data formatting | bytes 8388608
Async XLA Ops:
  99.8 3.3 %copy-start = (bf16[1024,2048]{1,0:T(8,128)(2,1)S(1)}, bf16[1024,2048]{1,0:T(8,128)(2,1)}, u32[]{:S(2)}) copy-start(bf16[1024,2048]{1,0:T(8,128)(2,1)} %get-tuple-element.5) | copy-start | bytes 12582916

commit v4 on v3

--- a/solution.py
+++ b/solution.py
@@ -315,7 +315,7 @@
     def logit_errors(w):
         rows = slice(w * HALF, (w + 1) * HALF)
 
-        @pl.loop(0, 4)
+        @pl.loop(0, 4, unroll=2)
         def _(k):
             cols = pl.ds(pl.multiple_of(k * BLOCK, BLOCK), BLOCK)
             weight = wh[:, :, :, :, :, cols].reshape(4096, BLOCK)
@@ -385,7 +385,7 @@
         if w == 0:
             send_errors(0, HALF)
         else:
-            send_errors(HALF, 48)
+            send_errors(HALF, HALF)
             backs[0].sum_second()
         backs[w].sum_first(ALL)
         h_mate.append(send(h1.at[w, mate], h2n.at[w, core], to_mate))
@@ -395,10 +395,8 @@
         if w == 0:
             e_large = [gather_large(FAR, e_small[v], h2f.at[v], 2) for v in range(2)]
     backs[0].sum_third()
-    send_errors(HALF + 48, 64)
     backs[1].sum_second()
     backs[1].sum_third()
-    send_errors(HALF + 112, 16)
     for wave in backs:
         wave.gather_second()
     for wave in backs:

time: 105 us -> 105 us (level)
  no operation moved by 1% of the time
where the time goes in v4:
time: 105 us
  Pallas kernels  99.2 us (94%)
  local copies, waits for them, and re-layouts  5.33 us (5%)
    pallas_call x1, Pallas kernels, body(): pl.pallas_call(kernel, out_shape=outs, in_specs=[hbm, hbm, hbm, vmem, vme...  99.2 us
    unnamed x4, local copies, waits for them, and re-layouts  5.33 us

profile of v4, /device:TPU:1, one launch (start us, length us, event | category | flops | bytes accessed | tf_op | source)
XLA Modules:
  0.0 105.2 jit_solution(3746461306310593250)
XLA Ops:
  0.6 99.2 %shard_map.86 = (f32[512,1024]{1,0:T(8,128)}, bf16[1024,2048]{1,0:T(8,128)(2,1)}) custom-call(bf16[256,512]{1,0:T(8,128)(2,1)} %feat_hbm.1, bf16[512,1024]{1,0:T(8,128)(2,1)} %wt_hbm.1, bf16[4,4,2,4,32,2048]{5,4,3,2,1,0:T(8,128)(2,1)} %bitcast.3, f32[32,128]{1,0:T(8,128)} %bitcast.4, f32[1,2048]{1,0:T(1,128)} %bitcast.5, bf16[256,2048]{1,0:T(8,128)(2,1)} %tg_hbm.1, ...), custom_call_target="tpu_custom_call" | custom-call | tf_op jit(solution)/shard_map/pallas_call | solution.py:464
  99.8 0.0 copy-start
  99.9 3.3 %copy.11 = f32[512,1024]{1,0:T(8,128)} copy(f32[512,1024]{1,0:T(8,128)} %get-tuple-element.4) | data formatting | bytes 4194304
  103.2 0.0 copy-done
  103.2 2.0 %copy.12 = bf16[1024,2048]{1,0:T(8,128)(2,1)} copy(bf16[1024,2048]{1,0:T(8,128)(2,1)S(1)} %copy-done) | data formatting | bytes 8388608
Async XLA Ops:
  99.8 3.3 %copy-start = (bf16[1024,2048]{1,0:T(8,128)(2,1)S(1)}, bf16[1024,2048]{1,0:T(8,128)(2,1)}, u32[]{:S(2)}) copy-start(bf16[1024,2048]{1,0:T(8,128)(2,1)} %get-tuple-element.5) | copy-start | bytes 12582916
